TPU v7x, 32 devices: a whole 2x2x4 slice. The times are simulated.
32 devices in a mesh: shell: 4 (over z), sky: 8 (over y, x, core).
Axes of the slice: x: 2, y: 2, z: 4, core: 2. Of those that a mesh axis runs over, the one named last changes fastest.
Arguments:
- density: bfloat16 [100, 384, 384], P('shell', 'sky'), may hold values from -6 to 6
- kernel_table: float32 [16, 4], replicated, may hold values from 0.02 to 0.4
- shell_row: int32 [100], P('shell'), may hold values from 0 to 15, as said below
- theta_first: bfloat16 [6, 4, 64], replicated, may hold values from -1.25 to 1.25
- bias_first: float32 [64], replicated, may hold values from -3 to 3
- theta_second: bfloat16 [6, 64, 64], replicated, may hold values from -0.3125 to 0.3125
- bias_second: float32 [64], replicated, may hold values from -3 to 3
Outputs:
- features: bfloat16 [64, 384, 384], P('shell', 'sky')
Inputs may be any that keep to these rules, and one draw needn't show every extreme that they name: `shell_row`: each shell names one row of kernel_table; both the first and the last row are named.
All inputs are finite; a program needn't handle non-finite values.
Results may differ from a plain program's by a relative error of at most 0.0062.
Values may be sent and summed in bfloat16 or wider, within the bound.
A program may use at most 128 MiB of HBM per device.

v0:
```python
import jax
import jax.numpy as jnp
from jax import lax
from jax.sharding import PartitionSpec as P


def padded(block, sides, width):
    for axis, dim in sides:
        count = lax.axis_size(axis)
        forward = [(i, i + 1) for i in range(count - 1)]
        forward.append((count - 1, 0))
        backward = [(target, source) for source, target in forward]
        low = lax.ppermute(
            lax.slice_in_dim(block, block.shape[dim] - width, None, axis=dim), axis, forward
        )
        high = lax.ppermute(lax.slice_in_dim(block, 0, width, axis=dim), axis, backward)
        block = jnp.concatenate([low, block, high], axis=dim)
    return block


def lateral(source_field):
    right_side = jnp.pad(source_field[:, :, 1:], ((0, 0), (0, 0), (0, 1)))
    left_side = jnp.pad(source_field[:, :, :-1], ((0, 0), (0, 0), (1, 0)))
    return right_side + left_side


def apply_rows(extended):
    return -0.25 * (extended[:, :-2] + extended[:, 2:] + lateral(extended[:, 1:-1]))


def basis_of(source_field, is_first, degrees):
    collected = [source_field.astype(jnp.bfloat16)]
    earlier = source_field.astype(jnp.float32)
    current = earlier
    for degree in range(1, degrees):
        if is_first:
            extended = padded(current, (("sky", 1),), 1)
        else:
            extended = padded(current, (("sky", 1),), 1)
        mapped = apply_rows(extended)
        if degree == 1:
            following = mapped
        else:
            following = 2.0 * mapped - earlier
        earlier = current
        current = following
        collected.append(following.astype(jnp.bfloat16))
    return jnp.stack(collected)


def per_device(
    density, kernel_table, shell_row, theta_first, bias_first, theta_second, bias_second
):
    degrees = theta_first.shape[0]
    table_rows = kernel_table.shape[0]
    table_ids = lax.broadcasted_iota(jnp.int32, (shell_row.shape[0], table_rows), 1)
    selector = (shell_row[:, None] == table_ids).astype(jnp.float32)
    weights = jnp.dot(selector, kernel_table, precision=lax.Precision.HIGHEST).astype(jnp.bfloat16)
    partial_sum = jnp.einsum("sb,syx->byx", weights, density, preferred_element_type=jnp.float32)
    convergence = lax.psum(partial_sum, "shell")
    first_basis = basis_of(convergence, True, degrees)
    groups = lax.axis_size("shell")
    shell_index = lax.axis_index("shell")
    width_out = theta_second.shape[2] // groups
    out_start = shell_index * width_out
    hidden = jnp.einsum(
        "kbo,kbyx->oyx", theta_first, first_basis, preferred_element_type=jnp.float32
    )
    hidden = jnp.maximum(hidden + bias_first[:, None, None], 0.0).astype(jnp.bfloat16)
    second_basis = basis_of(hidden, False, degrees)
    theta_cols = lax.dynamic_slice_in_dim(theta_second, out_start, width_out, 2)
    summed = jnp.einsum(
        "kio,kiyx->oyx", theta_cols, second_basis, preferred_element_type=jnp.float32
    )
    bias_cols = lax.dynamic_slice_in_dim(bias_second, out_start, width_out, 0)
    return (summed + bias_cols[:, None, None]).astype(jnp.bfloat16)


def solution(mesh):
    return jax.shard_map(
        per_device,
        mesh=mesh,
        in_specs=(P("shell", "sky", None), P(), P("shell"), P(), P(), P(), P()),
        out_specs=P("shell", "sky", None),
        check_vma=False,
    )
```

profile of v0, /device:TPU:0, one launch (start us, length us, event | category | flops | bytes accessed | tf_op | source)
XLA Modules:
  0.0 148.8 jit_solution(16323545694625500989)
XLA Ops:
  6.5 1.0 fusion.26
  7.5 0.2 copy-done
  7.7 1.0 fusion.24
  8.7 0.0 all-reduce.22.cloned.1.call-update
  8.8 0.7 dynamic_slice.7
  9.5 38.8 %all-reduce.22.cloned.1.call-done = f32[4,48,384]{2,0,1:T(4,128)} async-done(((f32[4,48,384]{2,0,1:T(4,128)}), f32[4,48,384]{2,0,1:T(4,128)}) %all-reduce.22.cloned.1.call-update) | async-done | bytes 294928 | tf_op jit(solution)/shard_map/psum | solution.py:60
  48.3 0.7 fusion.78
  49.0 2.6 %collective-permute-start.1 = (f32[4,1,384]{2,0,1:T(4,128)S(1)}, f32[4,1,384]{2,0,1:T(4,128)S(1)}, u32[]{:S(2)}, u32[]{:S(2)}) collective-permute-start(f32[4,1,384]{2,0,1:T(4,128)S(1)} %get-tuple-element.58), channel_id=1, source_target_pairs={{1,0},{2,1},{3,2},{4,3},{5,4},{6,5},{7,6},{0,7},{9,8},{10,9},{11,1... | collective-permute-start | bytes 18440 | tf_op jit(solution)/shard_map/ppermute | solution.py:16
  51.7 1.3 fusion.79
  52.9 1.0 bitcast_dynamic-update-slice_fusion.11
  54.0 1.3 bitcast_dynamic-update-slice_fusion.10
  55.3 0.1 collective-permute-start.2
  55.4 2.6 %collective-permute-start.3 = (f32[4,1,384]{2,0,1:T(4,128)S(1)}, f32[4,1,384]{2,0,1:T(4,128)S(1)}, u32[]{:S(2)}, u32[]{:S(2)}) collective-permute-start(f32[4,1,384]{2,0,1:T(4,128)S(1)} %get-tuple-element.54), channel_id=1, source_target_pairs={{1,0},{2,1},{3,2},{4,3},{5,4},{6,5},{7,6},{0,7},{9,8},{10,9},{11,1... | collective-permute-start | bytes 18440 | tf_op jit(solution)/shard_map/ppermute | solution.py:16
  58.0 0.2 fusion.77
  58.2 1.1 collective-permute-done.2
  59.3 0.0 collective-permute-done.3
  59.4 1.3 bitcast_dynamic-update-slice_fusion.9
  60.6 0.1 collective-permute-start.4
  60.8 2.6 %collective-permute-start.5 = (f32[4,1,384]{2,0,1:T(4,128)S(1)}, f32[4,1,384]{2,0,1:T(4,128)S(1)}, u32[]{:S(2)}, u32[]{:S(2)}) collective-permute-start(f32[4,1,384]{2,0,1:T(4,128)S(1)} %get-tuple-element.50), channel_id=1, source_target_pairs={{1,0},{2,1},{3,2},{4,3},{5,4},{6,5},{7,6},{0,7},{9,8},{10,9},{11,1... | collective-permute-start | bytes 18440 | tf_op jit(solution)/shard_map/ppermute | solution.py:16
  63.4 0.2 fusion.75
  63.6 1.1 collective-permute-done.4
  64.6 0.1 collective-permute-done.5
  64.7 0.3 bitcast_dynamic-update-slice_fusion.8
  65.0 0.5 collective-permute-start.6
  65.5 2.2 %collective-permute-start.7 = (f32[4,1,384]{2,0,1:T(4,128)S(1)}, f32[4,1,384]{2,0,1:T(4,128)S(1)}, u32[]{:S(2)}, u32[]{:S(2)}) collective-permute-start(f32[4,1,384]{2,0,1:T(4,128)S(1)} %get-tuple-element.46), channel_id=1, source_target_pairs={{1,0},{2,1},{3,2},{4,3},{5,4},{6,5},{7,6},{0,7},{9,8},{10,9},{11,1... | collective-permute-start | bytes 18440 | tf_op jit(solution)/shard_map/ppermute | solution.py:16
  67.7 0.2 fusion.73
  67.9 1.1 collective-permute-done.6
  69.0 0.1 collective-permute-done.7
  69.1 0.3 bitcast_dynamic-update-slice_fusion.7
  69.4 0.5 collective-permute-start.8
  69.8 2.2 %collective-permute-start.9 = (f32[4,1,384]{2,0,1:T(4,128)S(1)}, f32[4,1,384]{2,0,1:T(4,128)S(1)}, u32[]{:S(2)}, u32[]{:S(2)}) collective-permute-start(f32[4,1,384]{2,0,1:T(4,128)S(1)} %get-tuple-element.42), channel_id=1, source_target_pairs={{1,0},{2,1},{3,2},{4,3},{5,4},{6,5},{7,6},{0,7},{9,8},{10,9},{11,1... | collective-permute-start | bytes 18440 | tf_op jit(solution)/shard_map/ppermute | solution.py:16
  72.1 0.2 fusion.71
  72.3 1.1 collective-permute-done.8
  73.4 0.1 collective-permute-done.9
  73.4 0.3 bitcast_dynamic-update-slice_fusion.6
  73.7 2.5 %bitcast_dynamic-update-slice_fusion = (bf16[6,64,48,384]{3,1,2,0:T(8,128)(2,1)}, bf16[48,384,64]{1,2,0:T(8,128)(2,1)S(1)}) fusion(f32[64]{0:T(128)S(1)} %copy-done.5, bf16[6,4,48,384]{3,1,2,0:T(4,128)(2,1)S(1)} %bitcast_dynamic-update-slice_fusion.6, bf16[6,4,64]{2,1,0:T(4,128)(2,1)S(1)} %copy-done.4), kind=kOutput, calls=%fused_computation.33 | convolution fusion | flops 60162048 | bytes 5606656 | tf_op jit(solution)/shard_map/kbo,kbyx->oyx/dot_general | solution.py:66
  76.2 0.6 bitcast_convert_fusion
  76.8 0.5 collective-permute-start.10
  77.3 0.3 copy-done.2
  77.6 2.6 %collective-permute-start.11 = (f32[64,1,384]{2,0,1:T(8,128)S(1)}, f32[64,1,384]{2,0,1:T(8,128)S(1)}, u32[]{:S(2)}, u32[]{:S(2)}) collective-permute-start(f32[64,1,384]{2,0,1:T(8,128)S(1)} %get-tuple-element.38), channel_id=1, source_target_pairs={{1,0},{2,1},{3,2},{4,3},{5,4},{6,5},{7,6},{0,7},{9,8},{10,9},{11,1... | collective-permute-start | bytes 294920 | tf_op jit(solution)/shard_map/ppermute | solution.py:16
  80.2 1.8 %fusion.69 = (f32[64,48,383]{2,0,1:T(8,128)S(1)}, f32[64,48,383]{2,0,1:T(8,128)S(1)}) fusion(f32[64,48,384]{2,0,1:T(8,128)S(1)} %bitcast_convert_fusion), kind=kLoop, calls=%fused_computation.98 | loop fusion | bytes 18825216 | tf_op jit(solution)/shard_map/slice | solution.py:22
  82.0 0.2 collective-permute-done.10
  82.2 0.2 collective-permute-done.11
  82.4 3.7 %bitcast_dynamic-update-slice_fusion.5 = (bf16[6,64,48,384]{3,1,2,0:T(8,128)(2,1)}, f32[64,48,384]{2,0,1:T(8,128)S(1)}) fusion(bf16[6,64,48,384]{3,1,2,0:T(8,128)(2,1)} %get-tuple-element.61, f32[64,48,383]{2,0,1:T(8,128)S(1)} %get-tuple-element.40, f32[64,48,383]{2,0,1:T(8,128)S(1)} %get-tuple-element.39, f32[64,1,384]{2,0,1:T(8,128)S(1)} %collective-permute-done.11, ...), kind=kLoop, calls=%fused_computation.38 | loop fusion | flops 8257536 | bytes 21405696
  86.1 0.4 collective-permute-start.12
  86.5 2.5 %collective-permute-start.13 = (f32[64,1,384]{2,0,1:T(8,128)S(1)}, f32[64,1,384]{2,0,1:T(8,128)S(1)}, u32[]{:S(2)}, u32[]{:S(2)}) collective-permute-start(f32[64,1,384]{2,0,1:T(8,128)S(1)} %get-tuple-element.34), channel_id=1, source_target_pairs={{1,0},{2,1},{3,2},{4,3},{5,4},{6,5},{7,6},{0,7},{9,8},{10,9},{11,1... | collective-permute-start | bytes 294920 | tf_op jit(solution)/shard_map/ppermute | solution.py:16
  89.0 1.8 %fusion.67 = (f32[64,48,383]{2,0,1:T(8,128)S(1)}, f32[64,48,383]{2,0,1:T(8,128)S(1)}) fusion(f32[64,48,384]{2,0,1:T(8,128)S(1)} %get-tuple-element.12), kind=kLoop, calls=%fused_computation.96 | loop fusion | bytes 18825216 | tf_op jit(solution)/shard_map/slice | solution.py:22
  90.8 0.8 collective-permute-done.12
  91.6 5.3 %bitcast_dynamic-update-slice_fusion.4 = (bf16[6,64,48,384]{3,1,2,0:T(8,128)(2,1)}, f32[64,48,384]{2,0,1:T(8,128)S(1)}) fusion(bf16[6,64,48,384]{3,1,2,0:T(8,128)(2,1)} %get-tuple-element.11, bf16[48,384,64]{1,2,0:T(8,128)(2,1)} %copy-done.2, f32[64,48,383]{2,0,1:T(8,128)S(1)} %get-tuple-element.36, f32[64,48,383]{2,0,1:T(8,128)S(1)} %get-tuple-element.35, ...), kind=kLoop, calls=%fused_computation.37 | loop fusion | flops 10616832 | bytes 23764992
  96.9 0.5 collective-permute-start.14
  97.4 2.2 %collective-permute-start.15 = (f32[64,1,384]{2,0,1:T(8,128)S(1)}, f32[64,1,384]{2,0,1:T(8,128)S(1)}, u32[]{:S(2)}, u32[]{:S(2)}) collective-permute-start(f32[64,1,384]{2,0,1:T(8,128)S(1)} %get-tuple-element.30), channel_id=1, source_target_pairs={{1,0},{2,1},{3,2},{4,3},{5,4},{6,5},{7,6},{0,7},{9,8},{10,9},{11,1... | collective-permute-start | bytes 294920 | tf_op jit(solution)/shard_map/ppermute | solution.py:16
  99.6 3.8 %fusion.65 = (f32[64,48,383]{2,0,1:T(8,128)S(1)}, f32[64,48,383]{2,0,1:T(8,128)}) fusion(f32[64,48,384]{2,0,1:T(8,128)S(1)} %get-tuple-element.10), kind=kLoop, calls=%fused_computation.94 | loop fusion | bytes 18825216 | tf_op jit(solution)/shard_map/slice | solution.py:22
  103.4 5.9 %bitcast_dynamic-update-slice_fusion.3 = (bf16[6,64,48,384]{3,1,2,0:T(8,128)(2,1)}, f32[64,48,384]{2,0,1:T(8,128)S(1)}) fusion(bf16[6,64,48,384]{3,1,2,0:T(8,128)(2,1)} %get-tuple-element.9, f32[64,48,384]{2,0,1:T(8,128)S(1)} %get-tuple-element.12, f32[64,48,383]{2,0,1:T(8,128)} %get-tuple-element.32, f32[64,48,383]{2,0,1:T(8,128)S(1)} %get-tuple-element.31, ...), kind=kLoop, calls=%fused_computation.36 | loop fusion | flops 9437184 | bytes 26136576
  109.4 0.1 collective-permute-start.16
  109.4 2.6 %collective-permute-start.17 = (f32[64,1,384]{2,0,1:T(8,128)S(1)}, f32[64,1,384]{2,0,1:T(8,128)S(1)}, u32[]{:S(2)}, u32[]{:S(2)}) collective-permute-start(f32[64,1,384]{2,0,1:T(8,128)S(1)} %get-tuple-element.26), channel_id=1, source_target_pairs={{1,0},{2,1},{3,2},{4,3},{5,4},{6,5},{7,6},{0,7},{9,8},{10,9},{11,1... | collective-permute-start | bytes 294920 | tf_op jit(solution)/shard_map/ppermute | solution.py:16
  112.1 3.8 %fusion.63 = (f32[64,48,383]{2,0,1:T(8,128)S(1)}, f32[64,48,383]{2,0,1:T(8,128)}) fusion(f32[64,48,384]{2,0,1:T(8,128)S(1)} %get-tuple-element.8), kind=kLoop, calls=%fused_computation.92 | loop fusion | bytes 18825216 | tf_op jit(solution)/shard_map/slice | solution.py:22
  115.9 5.8 %bitcast_dynamic-update-slice_fusion.2 = (bf16[6,64,48,384]{3,1,2,0:T(8,128)(2,1)}, f32[64,48,384]{2,0,1:T(8,128)S(1)}) fusion(bf16[6,64,48,384]{3,1,2,0:T(8,128)(2,1)} %get-tuple-element.7, f32[64,48,384]{2,0,1:T(8,128)S(1)} %get-tuple-element.10, f32[64,48,383]{2,0,1:T(8,128)} %get-tuple-element.28, f32[64,48,383]{2,0,1:T(8,128)S(1)} %get-tuple-element.27, ...), kind=kLoop, calls=%fused_computation.35 | loop fusion | flops 9437184 | bytes 26136576
  121.7 0.1 collective-permute-start.18
  121.8 2.6 %collective-permute-start.19 = (f32[64,1,384]{2,0,1:T(8,128)S(1)}, f32[64,1,384]{2,0,1:T(8,128)S(1)}, u32[]{:S(2)}, u32[]{:S(2)}) collective-permute-start(f32[64,1,384]{2,0,1:T(8,128)S(1)} %get-tuple-element.22), channel_id=1, source_target_pairs={{1,0},{2,1},{3,2},{4,3},{5,4},{6,5},{7,6},{0,7},{9,8},{10,9},{11,1... | collective-permute-start | bytes 294920 | tf_op jit(solution)/shard_map/ppermute | solution.py:16
  124.4 3.8 %fusion.61 = (f32[64,48,383]{2,0,1:T(8,128)S(1)}, f32[64,48,383]{2,0,1:T(8,128)}) fusion(f32[64,48,384]{2,0,1:T(8,128)S(1)} %get-tuple-element.6), kind=kLoop, calls=%fused_computation.90 | loop fusion | bytes 18825216 | tf_op jit(solution)/shard_map/slice | solution.py:22
  128.2 0.0 copy-start.1
  128.2 5.7 %bitcast_dynamic-update-slice_fusion.1 = bf16[6,64,48,384]{3,1,2,0:T(8,128)(2,1)} fusion(bf16[6,64,48,384]{3,1,2,0:T(8,128)(2,1)} %get-tuple-element.5, f32[64,48,384]{2,0,1:T(8,128)S(1)} %get-tuple-element.8, f32[64,48,383]{2,0,1:T(8,128)} %get-tuple-element.24, f32[64,48,383]{2,0,1:T(8,128)S(1)} %get-tuple-element.23, ...), kind=kLoop, calls=%fused_computation.34 | loop fusion | flops 9437184 | bytes 21417984 | tf_op jit(solution)/shard_map/stack | solution.py:48
  133.9 7.1 %fusion.23 = bf16[16,48,384]{2,0,1:T(8,128)(2,1)S(1)} fusion(bf16[6,64,48,384]{3,1,2,0:T(8,128)(2,1)} %bitcast_dynamic-update-slice_fusion.1, f32[16]{0:T(128)S(1)} %dynamic_slice.7, bf16[6,64,64]{2,1,0:T(8,128)(2,1)S(1)} %copy-done.3, s32[]{:T(128)S(6)} %select_n.4), kind=kOutput, calls=%fused_computation.42 | convolution fusion | flops 227082240 | bytes 14794820 | tf_op jit(solution)/shard_map/kio,kiyx->oyx/dot_general | solution.py:72
  141.0 0.9 copy.13
  (29 shorter events, 0.1 us)
Async XLA Ops:
  6.5 1.2 copy-start
  6.5 41.8 %all-reduce.22.cloned.1.call-start = ((), (), s32[]{:S(2)}) async-start(), calls=%async_computation | async-start | bytes 589824 | tf_op jit(solution)/shard_map/psum | solution.py:60
  49.0 4.9 %collective-permute-start = (f32[4,1,384]{2,0,1:T(4,128)S(1)}, f32[4,1,384]{2,0,1:T(4,128)S(1)}, u32[]{:S(2)}, u32[]{:S(2)}) collective-permute-start(f32[4,1,384]{2,0,1:T(4,128)S(1)} %get-tuple-element.57), channel_id=1, source_target_pairs={{0,1},{1,2},{2,3},{3,4},{4,5},{5,6},{6,7},{7,0},{8,9},{9,10},{10,1... | collective-permute-start | bytes 18440 | tf_op jit(solution)/shard_map/ppermute | solution.py:13
  49.0 4.9 %collective-permute-start.1 = (f32[4,1,384]{2,0,1:T(4,128)S(1)}, f32[4,1,384]{2,0,1:T(4,128)S(1)}, u32[]{:S(2)}, u32[]{:S(2)}) collective-permute-start(f32[4,1,384]{2,0,1:T(4,128)S(1)} %get-tuple-element.58), channel_id=1, source_target_pairs={{1,0},{2,1},{3,2},{4,3},{5,4},{6,5},{7,6},{0,7},{9,8},{10,9},{11,1... | collective-permute-start | bytes 18440 | tf_op jit(solution)/shard_map/ppermute | solution.py:16
  55.3 4.0 %collective-permute-start.2 = (f32[4,1,384]{2,0,1:T(4,128)S(1)}, f32[4,1,384]{2,0,1:T(4,128)S(1)}, u32[]{:S(2)}, u32[]{:S(2)}) collective-permute-start(f32[4,1,384]{2,0,1:T(4,128)S(1)} %get-tuple-element.53), channel_id=1, source_target_pairs={{0,1},{1,2},{2,3},{3,4},{4,5},{5,6},{6,7},{7,0},{8,9},{9,10},{10,1... | collective-permute-start | bytes 18440 | tf_op jit(solution)/shard_map/ppermute | solution.py:13
  55.4 4.0 %collective-permute-start.3 = (f32[4,1,384]{2,0,1:T(4,128)S(1)}, f32[4,1,384]{2,0,1:T(4,128)S(1)}, u32[]{:S(2)}, u32[]{:S(2)}) collective-permute-start(f32[4,1,384]{2,0,1:T(4,128)S(1)} %get-tuple-element.54), channel_id=1, source_target_pairs={{1,0},{2,1},{3,2},{4,3},{5,4},{6,5},{7,6},{0,7},{9,8},{10,9},{11,1... | collective-permute-start | bytes 18440 | tf_op jit(solution)/shard_map/ppermute | solution.py:16
  59.4 14.3 %copy-start.4 = (bf16[6,4,64]{2,1,0:T(4,128)(2,1)S(1)}, bf16[6,4,64]{2,1,0:T(4,128)(2,1)}, u32[]{:S(2)}) copy-start(bf16[6,4,64]{2,1,0:T(4,128)(2,1)} %param.10) | copy-start | bytes 9220
  59.4 14.3 %copy-start.5 = (f32[64]{0:T(128)S(1)}, f32[64]{0:T(128)}, u32[]{:S(2)}) copy-start(f32[64]{0:T(128)} %param.11) | copy-start | bytes 772
  60.6 4.0 %collective-permute-start.4 = (f32[4,1,384]{2,0,1:T(4,128)S(1)}, f32[4,1,384]{2,0,1:T(4,128)S(1)}, u32[]{:S(2)}, u32[]{:S(2)}) collective-permute-start(f32[4,1,384]{2,0,1:T(4,128)S(1)} %get-tuple-element.49), channel_id=1, source_target_pairs={{0,1},{1,2},{2,3},{3,4},{4,5},{5,6},{6,7},{7,0},{8,9},{9,10},{10,1... | collective-permute-start | bytes 18440 | tf_op jit(solution)/shard_map/ppermute | solution.py:13
  60.8 4.0 %collective-permute-start.5 = (f32[4,1,384]{2,0,1:T(4,128)S(1)}, f32[4,1,384]{2,0,1:T(4,128)S(1)}, u32[]{:S(2)}, u32[]{:S(2)}) collective-permute-start(f32[4,1,384]{2,0,1:T(4,128)S(1)} %get-tuple-element.50), channel_id=1, source_target_pairs={{1,0},{2,1},{3,2},{4,3},{5,4},{6,5},{7,6},{0,7},{9,8},{10,9},{11,1... | collective-permute-start | bytes 18440 | tf_op jit(solution)/shard_map/ppermute | solution.py:16
  65.0 4.0 %collective-permute-start.6 = (f32[4,1,384]{2,0,1:T(4,128)S(1)}, f32[4,1,384]{2,0,1:T(4,128)S(1)}, u32[]{:S(2)}, u32[]{:S(2)}) collective-permute-start(f32[4,1,384]{2,0,1:T(4,128)S(1)} %get-tuple-element.45), channel_id=1, source_target_pairs={{0,1},{1,2},{2,3},{3,4},{4,5},{5,6},{6,7},{7,0},{8,9},{9,10},{10,1... | collective-permute-start | bytes 18440 | tf_op jit(solution)/shard_map/ppermute | solution.py:13
  65.5 3.6 %collective-permute-start.7 = (f32[4,1,384]{2,0,1:T(4,128)S(1)}, f32[4,1,384]{2,0,1:T(4,128)S(1)}, u32[]{:S(2)}, u32[]{:S(2)}) collective-permute-start(f32[4,1,384]{2,0,1:T(4,128)S(1)} %get-tuple-element.46), channel_id=1, source_target_pairs={{1,0},{2,1},{3,2},{4,3},{5,4},{6,5},{7,6},{0,7},{9,8},{10,9},{11,1... | collective-permute-start | bytes 18440 | tf_op jit(solution)/shard_map/ppermute | solution.py:16
  69.4 4.0 %collective-permute-start.8 = (f32[4,1,384]{2,0,1:T(4,128)S(1)}, f32[4,1,384]{2,0,1:T(4,128)S(1)}, u32[]{:S(2)}, u32[]{:S(2)}) collective-permute-start(f32[4,1,384]{2,0,1:T(4,128)S(1)} %get-tuple-element.41), channel_id=1, source_target_pairs={{0,1},{1,2},{2,3},{3,4},{4,5},{5,6},{6,7},{7,0},{8,9},{9,10},{10,1... | collective-permute-start | bytes 18440 | tf_op jit(solution)/shard_map/ppermute | solution.py:13
  69.8 3.6 %collective-permute-start.9 = (f32[4,1,384]{2,0,1:T(4,128)S(1)}, f32[4,1,384]{2,0,1:T(4,128)S(1)}, u32[]{:S(2)}, u32[]{:S(2)}) collective-permute-start(f32[4,1,384]{2,0,1:T(4,128)S(1)} %get-tuple-element.42), channel_id=1, source_target_pairs={{1,0},{2,1},{3,2},{4,3},{5,4},{6,5},{7,6},{0,7},{9,8},{10,9},{11,1... | collective-permute-start | bytes 18440 | tf_op jit(solution)/shard_map/ppermute | solution.py:16
  76.2 1.4 copy-start.2
  76.8 5.4 %collective-permute-start.10 = (f32[64,1,384]{2,0,1:T(8,128)S(1)}, f32[64,1,384]{2,0,1:T(8,128)S(1)}, u32[]{:S(2)}, u32[]{:S(2)}) collective-permute-start(f32[64,1,384]{2,0,1:T(8,128)S(1)} %get-tuple-element.37), channel_id=1, source_target_pairs={{0,1},{1,2},{2,3},{3,4},{4,5},{5,6},{6,7},{7,0},{8,9},{9,10},{10,1... | collective-permute-start | bytes 294920 | tf_op jit(solution)/shard_map/ppermute | solution.py:13
  77.6 4.8 %collective-permute-start.11 = (f32[64,1,384]{2,0,1:T(8,128)S(1)}, f32[64,1,384]{2,0,1:T(8,128)S(1)}, u32[]{:S(2)}, u32[]{:S(2)}) collective-permute-start(f32[64,1,384]{2,0,1:T(8,128)S(1)} %get-tuple-element.38), channel_id=1, source_target_pairs={{1,0},{2,1},{3,2},{4,3},{5,4},{6,5},{7,6},{0,7},{9,8},{10,9},{11,1... | collective-permute-start | bytes 294920 | tf_op jit(solution)/shard_map/ppermute | solution.py:16
  86.1 5.5 %collective-permute-start.12 = (f32[64,1,384]{2,0,1:T(8,128)S(1)}, f32[64,1,384]{2,0,1:T(8,128)S(1)}, u32[]{:S(2)}, u32[]{:S(2)}) collective-permute-start(f32[64,1,384]{2,0,1:T(8,128)S(1)} %get-tuple-element.33), channel_id=1, source_target_pairs={{0,1},{1,2},{2,3},{3,4},{4,5},{5,6},{6,7},{7,0},{8,9},{9,10},{10,1... | collective-permute-start | bytes 294920 | tf_op jit(solution)/shard_map/ppermute | solution.py:13
  86.5 5.1 %collective-permute-start.13 = (f32[64,1,384]{2,0,1:T(8,128)S(1)}, f32[64,1,384]{2,0,1:T(8,128)S(1)}, u32[]{:S(2)}, u32[]{:S(2)}) collective-permute-start(f32[64,1,384]{2,0,1:T(8,128)S(1)} %get-tuple-element.34), channel_id=1, source_target_pairs={{1,0},{2,1},{3,2},{4,3},{5,4},{6,5},{7,6},{0,7},{9,8},{10,9},{11,1... | collective-permute-start | bytes 294920 | tf_op jit(solution)/shard_map/ppermute | solution.py:16
  96.9 6.5 %collective-permute-start.14 = (f32[64,1,384]{2,0,1:T(8,128)S(1)}, f32[64,1,384]{2,0,1:T(8,128)S(1)}, u32[]{:S(2)}, u32[]{:S(2)}) collective-permute-start(f32[64,1,384]{2,0,1:T(8,128)S(1)} %get-tuple-element.29), channel_id=1, source_target_pairs={{0,1},{1,2},{2,3},{3,4},{4,5},{5,6},{6,7},{7,0},{8,9},{9,10},{10,1... | collective-permute-start | bytes 294920 | tf_op jit(solution)/shard_map/ppermute | solution.py:13
  97.4 6.0 %collective-permute-start.15 = (f32[64,1,384]{2,0,1:T(8,128)S(1)}, f32[64,1,384]{2,0,1:T(8,128)S(1)}, u32[]{:S(2)}, u32[]{:S(2)}) collective-permute-start(f32[64,1,384]{2,0,1:T(8,128)S(1)} %get-tuple-element.30), channel_id=1, source_target_pairs={{1,0},{2,1},{3,2},{4,3},{5,4},{6,5},{7,6},{0,7},{9,8},{10,9},{11,1... | collective-permute-start | bytes 294920 | tf_op jit(solution)/shard_map/ppermute | solution.py:16
  109.4 6.5 %collective-permute-start.16 = (f32[64,1,384]{2,0,1:T(8,128)S(1)}, f32[64,1,384]{2,0,1:T(8,128)S(1)}, u32[]{:S(2)}, u32[]{:S(2)}) collective-permute-start(f32[64,1,384]{2,0,1:T(8,128)S(1)} %get-tuple-element.25), channel_id=1, source_target_pairs={{0,1},{1,2},{2,3},{3,4},{4,5},{5,6},{6,7},{7,0},{8,9},{9,10},{10,1... | collective-permute-start | bytes 294920 | tf_op jit(solution)/shard_map/ppermute | solution.py:13
  109.4 6.4 %collective-permute-start.17 = (f32[64,1,384]{2,0,1:T(8,128)S(1)}, f32[64,1,384]{2,0,1:T(8,128)S(1)}, u32[]{:S(2)}, u32[]{:S(2)}) collective-permute-start(f32[64,1,384]{2,0,1:T(8,128)S(1)} %get-tuple-element.26), channel_id=1, source_target_pairs={{1,0},{2,1},{3,2},{4,3},{5,4},{6,5},{7,6},{0,7},{9,8},{10,9},{11,1... | collective-permute-start | bytes 294920 | tf_op jit(solution)/shard_map/ppermute | solution.py:16
  121.7 6.5 %collective-permute-start.18 = (f32[64,1,384]{2,0,1:T(8,128)S(1)}, f32[64,1,384]{2,0,1:T(8,128)S(1)}, u32[]{:S(2)}, u32[]{:S(2)}) collective-permute-start(f32[64,1,384]{2,0,1:T(8,128)S(1)} %get-tuple-element.21), channel_id=1, source_target_pairs={{0,1},{1,2},{2,3},{3,4},{4,5},{5,6},{6,7},{7,0},{8,9},{9,10},{10,1... | collective-permute-start | bytes 294920 | tf_op jit(solution)/shard_map/ppermute | solution.py:13
  121.8 6.4 %collective-permute-start.19 = (f32[64,1,384]{2,0,1:T(8,128)S(1)}, f32[64,1,384]{2,0,1:T(8,128)S(1)}, u32[]{:S(2)}, u32[]{:S(2)}) collective-permute-start(f32[64,1,384]{2,0,1:T(8,128)S(1)} %get-tuple-element.22), channel_id=1, source_target_pairs={{1,0},{2,1},{3,2},{4,3},{5,4},{6,5},{7,6},{0,7},{9,8},{10,9},{11,1... | collective-permute-start | bytes 294920 | tf_op jit(solution)/shard_map/ppermute | solution.py:16
  128.2 5.8 %copy-start.3 = (bf16[6,64,64]{2,1,0:T(8,128)(2,1)S(1)}, bf16[6,64,64]{2,1,0:T(8,128)(2,1)}, u32[]{:S(2)}) copy-start(bf16[6,64,64]{2,1,0:T(8,128)(2,1)} %param.12) | copy-start | bytes 147460
  128.2 13.7 %copy-start.1 = (bf16[25,48,384]{2,1,0:T(8,128)(2,1)S(1)}, bf16[25,48,384]{2,1,0:T(8,128)(2,1)}, u32[]{:S(2)}) copy-start(bf16[25,48,384]{2,1,0:T(8,128)(2,1)} %param.7) | copy-start | bytes 2764804
Sparse Core Ops, SparseCore 0:
  9.7 38.5 all-reduce.21
where the time goes:
time: 149 us
  waiting for transfers between devices  44.6 us (30%)
  other arithmetic  31.4 us (21%)
  starting transfers between devices  27.5 us (18%)
  local copies, waits for them, and re-layouts  20.1 us (13%)
  between operations  13.6 us (9%)
  matrix products  11.5 us (8%)
    psum x1, waiting for transfers between devices, per_device(): convergence = lax.psum(partial_sum, 'shell')  38.8 us
    ppermute x10, starting transfers between devices, padded(): lax.ppermute(lax.slice_in_dim(block, 0, width, axis=dim), axis, backward)  24.9 us
    unnamed x9, other arithmetic  24.8 us
    slice x10, local copies, waits for them, and re-layouts, lateral(): right_side = jnp.pad(source_field[:, :, 1:], ((0, 0), (0, 0), (0, 1)))  17.1 us
    dot_general x1, matrix products, per_device(): jnp.einsum('kio,kiyx->oyx', theta_cols, second_basis, preferred_element_t...  7.06 us
    another operation x2, other arithmetic, basis_of(): return jnp.stack(collected)  5.99 us
    ppermute x10, waiting for transfers between devices, padded(): lax.ppermute(lax.slice_in_dim(block, block.shape[dim] - width, None, axis...  5.37 us
  transfers between devices with their start and end apart: 21, of which 11 were waited for; matrix products, arithmetic and copies ran while one was open for 13% of the time, Pallas kernels for 0%

commit v1 on v0

v1 whole, which is shorter than its diff:
```python
import functools

import jax
import jax.numpy as jnp
from jax import lax
from jax.experimental import pallas as pl
from jax.experimental.pallas import tpu as pltpu
from jax.sharding import PartitionSpec as P

MESH = pl.DeviceIdType.MESH
EDGE = 16


def exchange_kernel(
    groups, tiles, density_hbm, table_ref, row_ref, ext_ref,
    dens, part, own, got, load_sem, rs_send, rs_recv, ag_send, ag_recv, up_send, up_recv, dn_send, dn_recv,
):
    me = lax.axis_index("shell")
    tile = lax.axis_index("sky")
    above = lax.rem(tile + tiles - 1, tiles)
    below = lax.rem(tile + 1, tiles)
    shells, rows, width = dens.shape
    bins = part.shape[0]
    load = pltpu.make_async_copy(density_hbm, dens, load_sem)
    load.start()
    barrier = pltpu.get_barrier_semaphore()
    for step in range(1, groups):
        pl.semaphore_signal(barrier, inc=1, device_id=(lax.rem(me + step, groups), tile), device_id_type=MESH)
    for group in range(groups):
        pl.semaphore_signal(barrier, inc=1, device_id=(group, above), device_id_type=MESH)
        pl.semaphore_signal(barrier, inc=1, device_id=(group, below), device_id_type=MESH)
    load.wait()

    def rounded(shell, b):
        weight = table_ref[row_ref[shell], b]
        return jnp.full((8, width), weight, jnp.float32).astype(jnp.bfloat16).astype(jnp.float32)

    block = 16

    def chunk(index, _):
        start = pl.multiple_of(index * block, block)
        sums = [jnp.zeros((block // 8, 8, width), jnp.float32) for _ in range(bins)]

        def add(shell, sums):
            field = dens[shell, pl.ds(start, block), :].astype(jnp.float32).reshape(block // 8, 8, width)
            return tuple(sums[b] + rounded(shell, b)[None] * field for b in range(bins))

        sums = lax.fori_loop(0, shells, add, tuple(sums), unroll=5 if shells % 5 == 0 else 1)
        for b in range(bins):
            total = sums[b].reshape(block, width)
            own[b, pl.ds(start, block), :] = total
            part[b, pl.ds(start, block), :] = total.astype(jnp.bfloat16)
        return 0

    lax.fori_loop(0, rows // block, chunk, 0)
    pl.semaphore_wait(barrier, groups - 1 + 2 * groups)

    reduce_copies = []
    for step in range(1, groups):
        peer = lax.rem(me + step, groups)
        copy = pltpu.make_async_remote_copy(
            src_ref=part.at[peer], dst_ref=got.at[step - 1],
            send_sem=rs_send.at[step - 1], recv_sem=rs_recv.at[step - 1],
            device_id=(peer, tile), device_id_type=MESH)
        copy.start()
        reduce_copies.append(copy)
    for copy in reduce_copies:
        copy.wait_recv()
    total = own[me]
    for step in range(groups - 1):
        total = total + got[step].astype(jnp.float32)
    ext_ref[me, EDGE:EDGE + rows, :] = total.astype(jnp.bfloat16)

    copies = []
    for step in range(1, groups):
        peer = lax.rem(me + step, groups)
        copies.append(pltpu.make_async_remote_copy(
            src_ref=ext_ref.at[me, pl.ds(EDGE, rows)], dst_ref=ext_ref.at[me, pl.ds(EDGE, rows)],
            send_sem=ag_send.at[step - 1], recv_sem=ag_recv.at[me],
            device_id=(peer, tile), device_id_type=MESH))
    for step in range(groups):
        peer = lax.rem(me + step, groups)
        copies.append(pltpu.make_async_remote_copy(
            src_ref=ext_ref.at[me, pl.ds(EDGE, EDGE)], dst_ref=ext_ref.at[me, pl.ds(EDGE + rows, EDGE)],
            send_sem=up_send.at[step], recv_sem=up_recv.at[me],
            device_id=(peer, above), device_id_type=MESH))
        copies.append(pltpu.make_async_remote_copy(
            src_ref=ext_ref.at[me, pl.ds(rows, EDGE)], dst_ref=ext_ref.at[me, pl.ds(0, EDGE)],
            send_sem=dn_send.at[step], recv_sem=dn_recv.at[me],
            device_id=(peer, below), device_id_type=MESH))
    for copy in copies:
        copy.start()
    for step in range(groups):
        peer = lax.rem(me + step, groups)
        if step > 0:
            pltpu.make_async_remote_copy(
                src_ref=ext_ref.at[peer, pl.ds(EDGE, rows)], dst_ref=ext_ref.at[peer, pl.ds(EDGE, rows)],
                send_sem=ag_send.at[step - 1], recv_sem=ag_recv.at[peer],
                device_id=(peer, tile), device_id_type=MESH).wait_recv()
        pltpu.make_async_remote_copy(
            src_ref=ext_ref.at[peer, pl.ds(EDGE, EDGE)], dst_ref=ext_ref.at[peer, pl.ds(EDGE + rows, EDGE)],
            send_sem=up_send.at[step], recv_sem=up_recv.at[peer],
            device_id=(peer, below), device_id_type=MESH).wait_recv()
        pltpu.make_async_remote_copy(
            src_ref=ext_ref.at[peer, pl.ds(rows, EDGE)], dst_ref=ext_ref.at[peer, pl.ds(0, EDGE)],
            send_sem=dn_send.at[step], recv_sem=dn_recv.at[peer],
            device_id=(peer, above), device_id_type=MESH).wait_recv()
    for copy in reduce_copies + copies:
        copy.wait_send()


def exchange(density, kernel_table, shell_row):
    groups = lax.axis_size("shell")
    tiles = lax.axis_size("sky")
    shells, rows, width = density.shape
    bins = kernel_table.shape[1]
    dma = pltpu.SemaphoreType.DMA
    return pl.pallas_call(
        functools.partial(exchange_kernel, groups, tiles),
        out_shape=jax.ShapeDtypeStruct((bins, rows + 2 * EDGE, width), jnp.bfloat16),
        in_specs=[
            pl.BlockSpec(memory_space=pl.ANY),
            pl.BlockSpec(memory_space=pltpu.SMEM),
            pl.BlockSpec(memory_space=pltpu.SMEM),
        ],
        out_specs=pl.BlockSpec(memory_space=pltpu.VMEM),
        scratch_shapes=[
            pltpu.VMEM((shells, rows, width), jnp.bfloat16),
            pltpu.VMEM((bins, rows, width), jnp.bfloat16),
            pltpu.VMEM((bins, rows, width), jnp.float32),
            pltpu.VMEM((groups - 1, rows, width), jnp.bfloat16),
            dma, dma((groups - 1,)), dma((groups - 1,)), dma((groups - 1,)), dma((groups,)),
            dma((groups,)), dma((groups,)), dma((groups,)), dma((groups,)),
        ],
        compiler_params=pltpu.CompilerParams(
            collective_id=0, has_side_effects=True, vmem_limit_bytes=16 * 2**20),
        cost_estimate=pl.CostEstimate(flops=2 * shells * bins * rows * width, bytes_accessed=2 * density.size, transcendentals=0),
    )(density, kernel_table, shell_row)


def conv_kernel(degrees, ext_ref, w1_ref, w2_ref, bias_ref, out_ref, basis, mixed, result):
    bins, span, width = ext_ref.shape
    outs, rows, _ = out_ref.shape
    half = rows // 2
    reach = degrees - 1
    need = half + 2 * reach
    lead = EDGE - 2 * reach
    base = EDGE - reach
    lane8 = lax.broadcasted_iota(jnp.int32, (8, width), 1)

    def lateral(field):
        flat = field.reshape(-1, width)
        lane = lax.broadcasted_iota(jnp.int32, flat.shape, 1)
        right = jnp.where(lane == width - 1, 0.0, pltpu.roll(flat, width - 1, 1))
        left = jnp.where(lane == 0, 0.0, pltpu.roll(flat, 1, 1))
        return (right + left).reshape(field.shape)

    for start in range(0, half + 2 * EDGE, 8):
        pieces = []
        for h in range(2):
            for b in range(bins):
                first = h * half + start
                low = first // 16 * 16
                tall = ext_ref[b, low:low + 16, :].astype(jnp.float32)
                pieces.append(tall[first - low:first - low + 8])
        basis[0, start:start + 8] = jnp.swapaxes(jnp.stack(pieces), 0, 1)

    step = 2
    for k in range(1, degrees):
        first = lead + k
        last = first + half + 4 * reach - 2 * k
        for r in range(first, last, step):
            n = min(step, last - r)
            total = basis[k - 1, r - 1:r - 1 + n] + basis[k - 1, r + 1:r + 1 + n] + lateral(basis[k - 1, r:r + n])
            if k == 1:
                basis[k, r:r + n] = -0.25 * total
            else:
                basis[k, r:r + n] = -0.5 * total - basis[k - 2, r:r + n]

    ones = jnp.ones((16, width), jnp.float32)
    w1 = w1_ref[...]
    w2 = w2_ref[...]
    deep = w2.shape[0] // degrees

    def mix(pair, _):
        columns = []
        for q in range(2):
            row = base + 2 * pair + q
            columns.append(jnp.concatenate([basis[k, row] for k in range(degrees)] + [ones], axis=0))
        operand = jnp.concatenate(columns, axis=1).astype(jnp.bfloat16)
        hidden = jnp.dot(w1, operand, preferred_element_type=jnp.float32)
        hidden = jnp.maximum(hidden, 0.0).astype(jnp.bfloat16)
        u = jnp.dot(w2, hidden, preferred_element_type=jnp.float32)
        for q in range(2):
            for k in range(degrees):
                mixed[k, 2 * pair + q] = u[k * deep:(k + 1) * deep, q * width:(q + 1) * width]
        return 0

    lax.fori_loop(0, need // 2, mix, 0)

    for k in range(degrees - 2, 0, -1):
        first = degrees - 1 - k

        def clenshaw(i, _, k=k, first=first):
            r = first + i
            total = mixed[k + 1, r - 1] + mixed[k + 1, r + 1] + lateral(mixed[k + 1, r])
            value = mixed[k, r] - 0.5 * total
            if k + 2 < degrees:
                value = value - mixed[k + 2, r]
            mixed[k, r] = value
            return 0

        lax.fori_loop(0, need - 2 * first, clenshaw, 0, unroll=2)

    def finish(block, _):
        values = []
        for i in range(8):
            r = reach + block * 8 + i
            total = mixed[1, r - 1] + mixed[1, r + 1] + lateral(mixed[1, r])
            values.append(mixed[0, r] - 0.25 * total - mixed[2, r])
        stacked = jnp.stack(values)
        for h in range(2):
            start = pl.multiple_of(h * half + block * 8, 8)
            result[:, pl.ds(start, 8), :] = jnp.swapaxes(stacked[:, h * outs:(h + 1) * outs], 0, 1)
        return 0

    lax.fori_loop(0, half // 8, finish, 0)
    shell = lax.axis_index("shell")
    for o in range(outs):
        out_ref[o] = (result[o] + bias_ref[shell * outs + o]).astype(jnp.bfloat16)


def three_parts(values):
    high = lax.reduce_precision(values, 8, 7)
    rest = values - high
    mid = lax.reduce_precision(rest, 8, 7)
    return jnp.stack([high, mid, rest - mid])


def per_device(
    density, kernel_table, shell_row, theta_first, bias_first, theta_second, bias_second
):
    degrees, bins, channels = theta_first.shape
    groups = lax.axis_size("shell")
    shell = lax.axis_index("shell")
    rows, width = density.shape[1:]
    outs = theta_second.shape[2] // groups

    eye = jnp.eye(2, dtype=jnp.bfloat16)
    w1 = jnp.einsum("kbo,hg->hokgb", theta_first, eye).reshape(2 * channels, degrees * 2 * bins)
    bias_cols = three_parts(bias_first).astype(jnp.bfloat16).T
    bias_cols = jnp.pad(jnp.concatenate([bias_cols, bias_cols]), ((0, 0), (0, 13)))
    w1 = jnp.concatenate([w1, bias_cols], axis=1)
    cols = lax.dynamic_slice_in_dim(theta_second, shell * outs, outs, 2)
    w2 = jnp.einsum("kio,hg->khogi", cols, eye).reshape(degrees * 2 * outs, 2 * channels)

    ext = exchange(density, kernel_table, shell_row)
    half = rows // 2
    need = half + 2 * (degrees - 1)
    vmem = pl.BlockSpec(memory_space=pltpu.VMEM)
    return pl.pallas_call(
        functools.partial(conv_kernel, degrees),
        out_shape=jax.ShapeDtypeStruct((outs, rows, width), jnp.bfloat16),
        in_specs=[vmem, vmem, vmem, pl.BlockSpec(memory_space=pltpu.SMEM)],
        out_specs=vmem,
        scratch_shapes=[
            pltpu.VMEM((degrees, half + 2 * EDGE, 2 * bins, width), jnp.float32),
            pltpu.VMEM((degrees, need, 2 * outs, width), jnp.float32),
            pltpu.VMEM((outs, rows, width), jnp.float32),
        ],
        compiler_params=pltpu.CompilerParams(vmem_limit_bytes=40 * 2**20),
    )(ext, w1, w2, bias_second)


def solution(mesh):
    return jax.shard_map(
        per_device,
        mesh=mesh,
        in_specs=(P("shell", "sky", None), P(), P("shell"), P(), P(), P(), P()),
        out_specs=P("shell", "sky", None),
        check_vma=False,
    )
```

time: 149 us -> 40.5 us (0.27)
  the two profiles are of different devices: /device:TPU:0 before, /device:TPU:1 now
where the time goes in v1:
time: 40.5 us; the launch traced here: 40.3 us
  Pallas kernels  36 us (89%)
  local copies, waits for them, and re-layouts  3.72 us (9%)
  other arithmetic  0.44 us (1%)
    pallas_call x1, Pallas kernels, exchange(): pl.pallas_call(functools.partial(exchange_kernel, groups, tiles), out_sha...  18.2 us
    pallas_call x1, Pallas kernels, per_device(): pl.pallas_call(functools.partial(conv_kernel, degrees), out_shape=jax.Sha...  17.8 us
    unnamed x15, local copies, waits for them, and re-layouts  2.98 us

profile of v1, /device:TPU:1, one launch (start us, length us, event | category | flops | bytes accessed | tf_op | source)
XLA Modules:
  0.0 40.3 jit_solution(8337153842712788744)
XLA Ops:
  0.0 0.0 copy-start
  0.0 0.0 copy-start.6
  0.0 0.1 copy.24
  0.1 0.6 %copy-done.6 = f32[64]{0:T(128)S(1)} copy-done((f32[64]{0:T(128)S(1)}, f32[64]{0:T(128)}, u32[]{:S(2)}) %copy-start.6) | copy-done | bytes 280
  0.7 0.0 copy-start.5
  0.7 0.0 copy-start.4
  0.7 0.1 pad_maximum_fusion
  0.8 0.6 %copy-done.5 = f32[16,4]{0,1:T(4,128)S(1)} copy-done((f32[16,4]{0,1:T(4,128)S(1)}, f32[16,4]{0,1:T(4,128)}, u32[]{:S(2)}) %copy-start.5) | copy-done | bytes 280
  1.4 0.1 copy.21.table_ref
  1.5 0.0 copy-done.4
  1.5 0.1 multiply_bitcast_fusion.1
  1.6 0.1 reshape.6
  1.7 0.1 copy.23
  1.8 0.1 copy.22
  1.9 0.1 fusion.1.w1_ref
  2.0 0.0 copy-done
  2.0 0.1 constant_dynamic-slice_fusion
  2.1 0.1 copy.25
  2.2 0.2 multiply_bitcast_fusion
  2.4 0.0 copy-start.2
  2.4 0.1 reshape.7.w2_ref
  2.5 0.5 %copy-done.2 = s32[25]{0:T(128)S(1)} copy-done((s32[25]{0:T(128)S(1)}, s32[25]{0:T(128)}, u32[]{:S(2)}) %copy-start.2) | copy-done | bytes 124
  3.1 0.0 copy-start.1
  3.1 1.2 %copy-done.1 = bf16[25,48,384]{2,1,0:T(8,128)(2,1)S(1)} copy-done((bf16[25,48,384]{2,1,0:T(8,128)(2,1)S(1)}, bf16[25,48,384]{2,1,0:T(8,128)(2,1)}, u32[]{:S(2)}) %copy-start.1) | copy-done | bytes 921624
  4.2 0.0 copy-start.3
  4.2 18.2 %shard_map.73.ext_ref = bf16[4,80,384]{2,1,0:T(8,128)(2,1)S(1)} custom-call(bf16[25,48,384]{2,1,0:T(8,128)(2,1)S(1)} %copy-done.1, f32[16,4]{1,0:T(8,128)S(1)} %copy.21.table_ref, s32[25]{0:T(128)S(1)} %copy-done.2), custom_call_target="tpu_custom_call" | custom-call | flops 3686400 | bytes 921600 | tf_op jit(solution)/shard_map/pallas_call | solution.py:118
  22.4 0.0 copy-done.3
  22.4 17.8 %shard_map.74 = bf16[16,48,384]{2,1,0:T(8,128)(2,1)} custom-call(bf16[4,80,384]{2,1,0:T(8,128)(2,1)S(1)} %shard_map.73.ext_ref, bf16[128,64]{1,0:T(8,128)(2,1)S(1)} %fusion.1.w1_ref, bf16[192,128]{1,0:T(8,128)(2,1)S(1)} %reshape.7.w2_ref, f32[64]{0:T(128)S(1)} %copy-done.3), custom_call_target="tpu_custom_call" | custom-call | tf_op jit(solution)/shard_map/pallas_call | solution.py:261
  (3 shorter events, 0.0 us)
Async XLA Ops:
  0.0 2.0 %copy-start = (bf16[6,64,64]{2,1,0:T(8,128)(2,1)S(1)}, bf16[6,64,64]{2,1,0:T(8,128)(2,1)}, u32[]{:S(2)}) copy-start(bf16[6,64,64]{2,1,0:T(8,128)(2,1)} %param.12) | copy-start | bytes 147460
  0.0 0.7 %copy-start.6 = (f32[64]{0:T(128)S(1)}, f32[64]{0:T(128)}, u32[]{:S(2)}) copy-start(f32[64]{0:T(128)} %param.11) | copy-start | bytes 772
  0.7 0.7 %copy-start.5 = (f32[16,4]{0,1:T(4,128)S(1)}, f32[16,4]{0,1:T(4,128)}, u32[]{:S(2)}) copy-start(f32[16,4]{0,1:T(4,128)} %param.8) | copy-start | bytes 772
  0.7 0.8 %copy-start.4 = (bf16[6,4,64]{2,1,0:T(4,128)(2,1)S(1)}, bf16[6,4,64]{2,1,0:T(4,128)(2,1)}, u32[]{:S(2)}) copy-start(bf16[6,4,64]{2,1,0:T(4,128)(2,1)} %param.10) | copy-start | bytes 9220
  2.4 0.7 %copy-start.2 = (s32[25]{0:T(128)S(1)}, s32[25]{0:T(128)}, u32[]{:S(2)}) copy-start(s32[25]{0:T(128)} %row_ref.1) | copy-start | bytes 304
  3.1 1.2 %copy-start.1 = (bf16[25,48,384]{2,1,0:T(8,128)(2,1)S(1)}, bf16[25,48,384]{2,1,0:T(8,128)(2,1)}, u32[]{:S(2)}) copy-start(bf16[25,48,384]{2,1,0:T(8,128)(2,1)} %density_hbm.1) | copy-start | bytes 2764804
  4.2 18.2 %copy-start.3 = (f32[64]{0:T(128)S(1)}, f32[64]{0:T(128)}, u32[]{:S(2)}) copy-start(f32[64]{0:T(128)} %bias_ref.1) | copy-start | bytes 772

commit v2 on v1

--- a/solution.py
+++ b/solution.py
@@ -9,6 +9,8 @@
 
 MESH = pl.DeviceIdType.MESH
 EDGE = 16
+CL = 1
+MIXU = True
 
 
 def exchange_kernel(
@@ -31,81 +33,81 @@
         pl.semaphore_signal(barrier, inc=1, device_id=(group, below), device_id_type=MESH)
     load.wait()
 
-    def rounded(shell, b):
-        weight = table_ref[row_ref[shell], b]
-        return jnp.full((8, width), weight, jnp.float32).astype(jnp.bfloat16).astype(jnp.float32)
-
-    block = 16
-
-    def chunk(index, _):
-        start = pl.multiple_of(index * block, block)
-        sums = [jnp.zeros((block // 8, 8, width), jnp.float32) for _ in range(bins)]
+    block = EDGE
+    chunks = rows // block
+    order = [0, chunks - 1] + list(range(1, chunks - 1))
+    per_trip = 5 if shells % 5 == 0 else 1
+    started = []
+    for turn, c in enumerate(order):
+        span = pl.ds(c * block, block)
 
         def add(shell, sums):
-            field = dens[shell, pl.ds(start, block), :].astype(jnp.float32).reshape(block // 8, 8, width)
-            return tuple(sums[b] + rounded(shell, b)[None] * field for b in range(bins))
-
-        sums = lax.fori_loop(0, shells, add, tuple(sums), unroll=5 if shells % 5 == 0 else 1)
+            field = dens[shell, c * block:(c + 1) * block, :].astype(jnp.float32)
+            return tuple(sums[b] + table_ref[row_ref[shell], b] * field for b in range(bins))
+
+        sums = tuple(jnp.zeros((block, width), jnp.float32) for _ in range(bins))
+        sums = lax.fori_loop(0, shells, add, sums, unroll=per_trip)
         for b in range(bins):
-            total = sums[b].reshape(block, width)
-            own[b, pl.ds(start, block), :] = total
-            part[b, pl.ds(start, block), :] = total.astype(jnp.bfloat16)
-        return 0
-
-    lax.fori_loop(0, rows // block, chunk, 0)
-    pl.semaphore_wait(barrier, groups - 1 + 2 * groups)
-
-    reduce_copies = []
-    for step in range(1, groups):
-        peer = lax.rem(me + step, groups)
-        copy = pltpu.make_async_remote_copy(
-            src_ref=part.at[peer], dst_ref=got.at[step - 1],
-            send_sem=rs_send.at[step - 1], recv_sem=rs_recv.at[step - 1],
+            own[b, c * block:(c + 1) * block, :] = sums[b]
+            part[b, c * block:(c + 1) * block, :] = sums[b].astype(jnp.bfloat16)
+        if turn == 0:
+            pl.semaphore_wait(barrier, groups - 1 + 2 * groups)
+        for step in range(1, groups):
+            peer = lax.rem(me + step, groups)
+            copy = pltpu.make_async_remote_copy(
+                src_ref=part.at[peer, span], dst_ref=got.at[step - 1, span],
+                send_sem=rs_send.at[step - 1, c], recv_sem=rs_recv.at[step - 1, c],
+                device_id=(peer, tile), device_id_type=MESH)
+            copy.start()
+            started.append(copy)
+
+    def gather_copy(owner, peer, c, sem):
+        place = ext_ref.at[owner, pl.ds(EDGE + c * block, block)]
+        return pltpu.make_async_remote_copy(
+            src_ref=place, dst_ref=place, send_sem=ag_send.at[sem, c], recv_sem=ag_recv.at[owner, c],
             device_id=(peer, tile), device_id_type=MESH)
-        copy.start()
-        reduce_copies.append(copy)
-    for copy in reduce_copies:
-        copy.wait_recv()
-    total = own[me]
-    for step in range(groups - 1):
-        total = total + got[step].astype(jnp.float32)
-    ext_ref[me, EDGE:EDGE + rows, :] = total.astype(jnp.bfloat16)
-
-    copies = []
-    for step in range(1, groups):
-        peer = lax.rem(me + step, groups)
-        copies.append(pltpu.make_async_remote_copy(
-            src_ref=ext_ref.at[me, pl.ds(EDGE, rows)], dst_ref=ext_ref.at[me, pl.ds(EDGE, rows)],
-            send_sem=ag_send.at[step - 1], recv_sem=ag_recv.at[me],
-            device_id=(peer, tile), device_id_type=MESH))
-    for step in range(groups):
-        peer = lax.rem(me + step, groups)
-        copies.append(pltpu.make_async_remote_copy(
-            src_ref=ext_ref.at[me, pl.ds(EDGE, EDGE)], dst_ref=ext_ref.at[me, pl.ds(EDGE + rows, EDGE)],
-            send_sem=up_send.at[step], recv_sem=up_recv.at[me],
-            device_id=(peer, above), device_id_type=MESH))
-        copies.append(pltpu.make_async_remote_copy(
-            src_ref=ext_ref.at[me, pl.ds(rows, EDGE)], dst_ref=ext_ref.at[me, pl.ds(0, EDGE)],
-            send_sem=dn_send.at[step], recv_sem=dn_recv.at[me],
-            device_id=(peer, below), device_id_type=MESH))
-    for copy in copies:
-        copy.start()
+
+    def up_copy(owner, peer, beside, sem):
+        return pltpu.make_async_remote_copy(
+            src_ref=ext_ref.at[owner, pl.ds(EDGE, EDGE)], dst_ref=ext_ref.at[owner, pl.ds(EDGE + rows, EDGE)],
+            send_sem=up_send.at[sem], recv_sem=up_recv.at[owner],
+            device_id=(peer, beside), device_id_type=MESH)
+
+    def down_copy(owner, peer, beside, sem):
+        return pltpu.make_async_remote_copy(
+            src_ref=ext_ref.at[owner, pl.ds(rows, EDGE)], dst_ref=ext_ref.at[owner, pl.ds(0, EDGE)],
+            send_sem=dn_send.at[sem], recv_sem=dn_recv.at[owner],
+            device_id=(peer, beside), device_id_type=MESH)
+
+    for turn, c in enumerate(order):
+        for step in range(1, groups):
+            started[turn * (groups - 1) + step - 1].wait_recv()
+        total = own[me, c * block:(c + 1) * block, :]
+        for step in range(groups - 1):
+            total = total + got[step, c * block:(c + 1) * block, :].astype(jnp.float32)
+        ext_ref[me, EDGE + c * block:EDGE + (c + 1) * block, :] = total.astype(jnp.bfloat16)
+        for step in range(groups - 1, -1, -1):
+            peer = lax.rem(me + step, groups)
+            if step > 0:
+                copy = gather_copy(me, peer, c, step - 1)
+                copy.start()
+                started.append(copy)
+            if c == 0:
+                copy = up_copy(me, peer, above, step)
+                copy.start()
+                started.append(copy)
+            if c == chunks - 1:
+                copy = down_copy(me, peer, below, step)
+                copy.start()
+                started.append(copy)
     for step in range(groups):
         peer = lax.rem(me + step, groups)
         if step > 0:
-            pltpu.make_async_remote_copy(
-                src_ref=ext_ref.at[peer, pl.ds(EDGE, rows)], dst_ref=ext_ref.at[peer, pl.ds(EDGE, rows)],
-                send_sem=ag_send.at[step - 1], recv_sem=ag_recv.at[peer],
-                device_id=(peer, tile), device_id_type=MESH).wait_recv()
-        pltpu.make_async_remote_copy(
-            src_ref=ext_ref.at[peer, pl.ds(EDGE, EDGE)], dst_ref=ext_ref.at[peer, pl.ds(EDGE + rows, EDGE)],
-            send_sem=up_send.at[step], recv_sem=up_recv.at[peer],
-            device_id=(peer, below), device_id_type=MESH).wait_recv()
-        pltpu.make_async_remote_copy(
-            src_ref=ext_ref.at[peer, pl.ds(rows, EDGE)], dst_ref=ext_ref.at[peer, pl.ds(0, EDGE)],
-            send_sem=dn_send.at[step], recv_sem=dn_recv.at[peer],
-            device_id=(peer, above), device_id_type=MESH).wait_recv()
-    for copy in reduce_copies + copies:
+            for c in range(chunks):
+                gather_copy(peer, peer, c, step - 1).wait_recv()
+        up_copy(peer, peer, below, step).wait_recv()
+        down_copy(peer, peer, above, step).wait_recv()
+    for copy in started:
         copy.wait_send()
 
 
@@ -115,6 +117,7 @@
     shells, rows, width = density.shape
     bins = kernel_table.shape[1]
     dma = pltpu.SemaphoreType.DMA
+    chunks = rows // EDGE
     return pl.pallas_call(
         functools.partial(exchange_kernel, groups, tiles),
         out_shape=jax.ShapeDtypeStruct((bins, rows + 2 * EDGE, width), jnp.bfloat16),
@@ -129,13 +132,13 @@
             pltpu.VMEM((bins, rows, width), jnp.bfloat16),
             pltpu.VMEM((bins, rows, width), jnp.float32),
             pltpu.VMEM((groups - 1, rows, width), jnp.bfloat16),
-            dma, dma((groups - 1,)), dma((groups - 1,)), dma((groups - 1,)), dma((groups,)),
+            dma, dma((groups - 1, chunks)), dma((groups - 1, chunks)), dma((groups - 1, chunks)), dma((groups, chunks)),
             dma((groups,)), dma((groups,)), dma((groups,)), dma((groups,)),
         ],
         compiler_params=pltpu.CompilerParams(
-            collective_id=0, has_side_effects=True, vmem_limit_bytes=16 * 2**20),
+            collective_id=0, has_side_effects=True, vmem_limit_bytes=56 * 2**20),
         cost_estimate=pl.CostEstimate(flops=2 * shells * bins * rows * width, bytes_accessed=2 * density.size, transcendentals=0),
-    )(density, kernel_table, shell_row)
+    )(density, lax.reduce_precision(kernel_table, 8, 7), shell_row)
 
 
 def conv_kernel(degrees, ext_ref, w1_ref, w2_ref, bias_ref, out_ref, basis, mixed, result):
@@ -146,7 +149,6 @@
     need = half + 2 * reach
     lead = EDGE - 2 * reach
     base = EDGE - reach
-    lane8 = lax.broadcasted_iota(jnp.int32, (8, width), 1)
 
     def lateral(field):
         flat = field.reshape(-1, width)
@@ -196,21 +198,23 @@
                 mixed[k, 2 * pair + q] = u[k * deep:(k + 1) * deep, q * width:(q + 1) * width]
         return 0
 
-    lax.fori_loop(0, need // 2, mix, 0)
+    lax.fori_loop(0, need // 2, mix, 0, unroll=MIXU)
 
     for k in range(degrees - 2, 0, -1):
         first = degrees - 1 - k
 
-        def clenshaw(i, _, k=k, first=first):
-            r = first + i
-            total = mixed[k + 1, r - 1] + mixed[k + 1, r + 1] + lateral(mixed[k + 1, r])
-            value = mixed[k, r] - 0.5 * total
+        def clenshaw(r, n, k=k):
+            value = mixed[k, pl.ds(r, n)] - 0.5 * (
+                mixed[k + 1, pl.ds(r - 1, n)] + mixed[k + 1, pl.ds(r + 1, n)] + lateral(mixed[k + 1, pl.ds(r, n)]))
             if k + 2 < degrees:
-                value = value - mixed[k + 2, r]
-            mixed[k, r] = value
-            return 0
-
-        lax.fori_loop(0, need - 2 * first, clenshaw, 0, unroll=2)
+                value = value - mixed[k + 2, pl.ds(r, n)]
+            mixed[k, pl.ds(r, n)] = value
+
+        count = need - 2 * first
+        for i in range(count // CL):
+            clenshaw(first + i * CL, CL)
+        if count % CL:
+            clenshaw(first + count // CL * CL, count % CL)
 
     def finish(block, _):
         values = []

time: 40.5 us -> 30.5 us (0.75)
  the two profiles are of different devices: /device:TPU:1 before, /device:TPU:0 now
where the time goes in v2:
time: 30.5 us; the launch traced here: 30.2 us
  Pallas kernels  26.1 us (86%)
  local copies, waits for them, and re-layouts  3.55 us (12%)
  other arithmetic  0.44 us (1%)
    pallas_call x1, Pallas kernels, exchange(): pl.pallas_call(functools.partial(exchange_kernel, groups, tiles), out_sha...  18.5 us
    pallas_call x1, Pallas kernels, per_device(): pl.pallas_call(functools.partial(conv_kernel, degrees), out_shape=jax.Sha...  7.57 us
    unnamed x12, local copies, waits for them, and re-layouts  2.12 us
    reduce_precision x1, local copies, waits for them, and re-layouts, exchange(): lax.reduce_precision(kernel_table, 8, 7)  0.68 us

profile of v2, /device:TPU:0, one launch (start us, length us, event | category | flops | bytes accessed | tf_op | source)
XLA Modules:
  0.0 30.2 jit_solution(15346244276802833089)
XLA Ops:
  0.0 0.0 copy-start
  0.0 0.0 copy-start.5
  0.0 0.1 copy.29
  0.1 0.6 %copy-done.5 = f32[64]{0:T(128)S(1)} copy-done((f32[64]{0:T(128)S(1)}, f32[64]{0:T(128)}, u32[]{:S(2)}) %copy-start.5) | copy-done | bytes 280
  0.7 0.0 copy-start.4
  0.7 0.1 pad_maximum_fusion
  0.8 0.6 %copy-done.4 = f32[16,4]{0,1:T(4,128)S(1)} copy-done((f32[16,4]{0,1:T(4,128)S(1)}, f32[16,4]{0,1:T(4,128)}, u32[]{:S(2)}) %copy-start.4) | copy-done | bytes 280
  1.4 0.0 copy-start.3
  1.4 0.7 %copy.26.table_ref = f32[16,4]{1,0:T(8,128)} copy(f32[16,4]{0,1:T(4,128)S(1)} %reduce_precision.9) | data formatting | bytes 512 | tf_op jit(solution)/shard_map/reduce_precision | solution.py:141
  2.1 0.0 copy-done.3
  2.1 0.1 multiply_bitcast_fusion.1
  2.2 0.1 reshape.6
  2.3 0.1 copy.28
  2.4 0.1 copy.27
  2.5 0.1 fusion.1.w1_ref
  2.6 0.0 copy-done
  2.6 0.1 constant_dynamic-slice_fusion
  2.7 0.1 copy.30
  2.8 0.2 multiply_bitcast_fusion
  3.0 0.1 reshape.7.w2_ref
  3.1 0.0 copy-start.2
  3.1 18.5 %shard_map.73.ext_ref = bf16[4,80,384]{2,1,0:T(8,128)(2,1)} custom-call(bf16[25,48,384]{2,1,0:T(8,128)(2,1)} %density_hbm.1, f32[16,4]{1,0:T(8,128)} %copy.26.table_ref, s32[25]{0:T(128)} %row_ref.1), custom_call_target="tpu_custom_call" | custom-call | flops 3686400 | bytes 921600 | tf_op jit(solution)/shard_map/pallas_call | solution.py:121
  21.6 0.0 copy-done.2
  21.6 0.0 copy-start.1
  21.7 0.9 %copy-done.1 = bf16[4,80,384]{2,1,0:T(8,128)(2,1)S(1)} copy-done((bf16[4,80,384]{2,1,0:T(8,128)(2,1)S(1)}, bf16[4,80,384]{2,1,0:T(8,128)(2,1)}, u32[]{:S(2)}) %copy-start.1) | copy-done | bytes 245784
  22.6 7.6 %shard_map.74 = bf16[16,48,384]{2,1,0:T(8,128)(2,1)} custom-call(bf16[4,80,384]{2,1,0:T(8,128)(2,1)S(1)} %copy-done.1, bf16[128,64]{1,0:T(8,128)(2,1)S(1)} %fusion.1.w1_ref, bf16[192,128]{1,0:T(8,128)(2,1)S(1)} %reshape.7.w2_ref, f32[64]{0:T(128)S(1)} %copy-done.2), custom_call_target="tpu_custom_call" | custom-call | tf_op jit(solution)/shard_map/pallas_call | solution.py:265
  (4 shorter events, 0.0 us)
Async XLA Ops:
  0.0 2.6 %copy-start = (bf16[6,64,64]{2,1,0:T(8,128)(2,1)S(1)}, bf16[6,64,64]{2,1,0:T(8,128)(2,1)}, u32[]{:S(2)}) copy-start(bf16[6,64,64]{2,1,0:T(8,128)(2,1)} %param.12) | copy-start | bytes 147460
  0.0 0.7 %copy-start.5 = (f32[64]{0:T(128)S(1)}, f32[64]{0:T(128)}, u32[]{:S(2)}) copy-start(f32[64]{0:T(128)} %param.11) | copy-start | bytes 772
  0.7 0.7 %copy-start.4 = (f32[16,4]{0,1:T(4,128)S(1)}, f32[16,4]{0,1:T(4,128)}, u32[]{:S(2)}) copy-start(f32[16,4]{0,1:T(4,128)} %param.8) | copy-start | bytes 772
  1.4 0.7 %copy-start.3 = (bf16[6,4,64]{2,1,0:T(4,128)(2,1)S(1)}, bf16[6,4,64]{2,1,0:T(4,128)(2,1)}, u32[]{:S(2)}) copy-start(bf16[6,4,64]{2,1,0:T(4,128)(2,1)} %param.10) | copy-start | bytes 9220
  3.1 18.5 %copy-start.2 = (f32[64]{0:T(128)S(1)}, f32[64]{0:T(128)}, u32[]{:S(2)}) copy-start(f32[64]{0:T(128)} %bias_ref.1) | copy-start | bytes 772
  21.6 0.9 %copy-start.1 = (bf16[4,80,384]{2,1,0:T(8,128)(2,1)S(1)}, bf16[4,80,384]{2,1,0:T(8,128)(2,1)}, u32[]{:S(2)}) copy-start(bf16[4,80,384]{2,1,0:T(8,128)(2,1)} %shard_map.73.ext_ref) | copy-start | bytes 737284

commit v3 on v2

--- a/solution.py
+++ b/solution.py
@@ -15,7 +15,7 @@
 
 def exchange_kernel(
     groups, tiles, density_hbm, table_ref, row_ref, ext_ref,
-    dens, part, own, got, load_sem, rs_send, rs_recv, ag_send, ag_recv, up_send, up_recv, dn_send, dn_recv,
+    dens, weights, part, own, got, load_sem, rs_send, rs_recv, ag_send, ag_recv, up_send, up_recv, dn_send, dn_recv,
 ):
     me = lax.axis_index("shell")
     tile = lax.axis_index("sky")
@@ -31,6 +31,10 @@
     for group in range(groups):
         pl.semaphore_signal(barrier, inc=1, device_id=(group, above), device_id_type=MESH)
         pl.semaphore_signal(barrier, inc=1, device_id=(group, below), device_id_type=MESH)
+    for b in range(bins):
+        for shell in range(shells):
+            weight = jnp.full((EDGE, 128), table_ref[b, row_ref[shell]], jnp.float32)
+            weights[shell, b] = weight.astype(jnp.bfloat16).astype(jnp.float32)[:8]
     load.wait()
 
     block = EDGE
@@ -43,7 +47,8 @@
 
         def add(shell, sums):
             field = dens[shell, c * block:(c + 1) * block, :].astype(jnp.float32)
-            return tuple(sums[b] + table_ref[row_ref[shell], b] * field for b in range(bins))
+            wide = [jnp.tile(weights[shell, b], (block // 8, width // 128)) for b in range(bins)]
+            return tuple(sums[b] + wide[b] * field for b in range(bins))
 
         sums = tuple(jnp.zeros((block, width), jnp.float32) for _ in range(bins))
         sums = lax.fori_loop(0, shells, add, sums, unroll=per_trip)
@@ -129,6 +134,7 @@
         out_specs=pl.BlockSpec(memory_space=pltpu.VMEM),
         scratch_shapes=[
             pltpu.VMEM((shells, rows, width), jnp.bfloat16),
+            pltpu.VMEM((shells, bins, 8, 128), jnp.float32),
             pltpu.VMEM((bins, rows, width), jnp.bfloat16),
             pltpu.VMEM((bins, rows, width), jnp.float32),
             pltpu.VMEM((groups - 1, rows, width), jnp.bfloat16),
@@ -136,19 +142,47 @@
             dma((groups,)), dma((groups,)), dma((groups,)), dma((groups,)),
         ],
         compiler_params=pltpu.CompilerParams(
-            collective_id=0, has_side_effects=True, vmem_limit_bytes=56 * 2**20),
+            collective_id=0, has_side_effects=True, vmem_limit_bytes=58 * 2**20),
         cost_estimate=pl.CostEstimate(flops=2 * shells * bins * rows * width, bytes_accessed=2 * density.size, transcendentals=0),
-    )(density, lax.reduce_precision(kernel_table, 8, 7), shell_row)
-
-
-def conv_kernel(degrees, ext_ref, w1_ref, w2_ref, bias_ref, out_ref, basis, mixed, result):
-    bins, span, width = ext_ref.shape
+    )(density, kernel_table.T, shell_row)
+
+
+def conv_kernel(ext_hbm, first_ref, lift_ref, second_ref, bias_ref, out_ref, ext_ref, basis, mixed, result, flat_first, turned, sem):
+    load = pltpu.make_async_copy(ext_hbm, ext_ref, sem)
+    load.start()
+    degrees, bins, channels = first_ref.shape
+    width = ext_ref.shape[2]
+    shell = lax.axis_index("shell")
     outs, rows, _ = out_ref.shape
     half = rows // 2
     reach = degrees - 1
     need = half + 2 * reach
     lead = EDGE - 2 * reach
     base = EDGE - reach
+
+    flat_first[...] = jnp.zeros_like(flat_first)
+    for h in range(2):
+        span = slice(h * channels, (h + 1) * channels)
+        for k in range(degrees):
+            row = (2 * k + h) * bins
+            flat_first[row:row + bins, span] = first_ref[k].astype(jnp.float32)
+        rest = lift_ref[...]
+        for part in range(3):
+            row = 2 * bins * degrees + part
+            high = rest.astype(jnp.bfloat16).astype(jnp.float32)
+            flat_first[row:row + 1, span] = high
+            rest = rest - high
+    w1 = flat_first[...].T.astype(jnp.bfloat16)
+    lanes = lax.broadcasted_iota(jnp.int32, (outs, 2 * channels), 1)
+    pieces = []
+    for k in range(degrees):
+        across = second_ref[k].astype(jnp.float32).T
+        turned[k] = jnp.concatenate([across, across], axis=1)
+        mine = turned[k, pl.ds(pl.multiple_of(shell * outs, outs), outs), :]
+        pieces.append(jnp.where(lanes < channels, mine, 0.0))
+        pieces.append(jnp.where(lanes < channels, 0.0, mine))
+    w2 = jnp.concatenate(pieces, axis=0).astype(jnp.bfloat16)
+    load.wait()
 
     def lateral(field):
         flat = field.reshape(-1, width)
@@ -180,8 +214,6 @@
                 basis[k, r:r + n] = -0.5 * total - basis[k - 2, r:r + n]
 
     ones = jnp.ones((16, width), jnp.float32)
-    w1 = w1_ref[...]
-    w2 = w2_ref[...]
     deep = w2.shape[0] // degrees
 
     def mix(pair, _):
@@ -229,16 +261,8 @@
         return 0
 
     lax.fori_loop(0, half // 8, finish, 0)
-    shell = lax.axis_index("shell")
     for o in range(outs):
         out_ref[o] = (result[o] + bias_ref[shell * outs + o]).astype(jnp.bfloat16)
-
-
-def three_parts(values):
-    high = lax.reduce_precision(values, 8, 7)
-    rest = values - high
-    mid = lax.reduce_precision(rest, 8, 7)
-    return jnp.stack([high, mid, rest - mid])
 
 
 def per_device(
@@ -246,34 +270,28 @@
 ):
     degrees, bins, channels = theta_first.shape
     groups = lax.axis_size("shell")
-    shell = lax.axis_index("shell")
     rows, width = density.shape[1:]
     outs = theta_second.shape[2] // groups
-
-    eye = jnp.eye(2, dtype=jnp.bfloat16)
-    w1 = jnp.einsum("kbo,hg->hokgb", theta_first, eye).reshape(2 * channels, degrees * 2 * bins)
-    bias_cols = three_parts(bias_first).astype(jnp.bfloat16).T
-    bias_cols = jnp.pad(jnp.concatenate([bias_cols, bias_cols]), ((0, 0), (0, 13)))
-    w1 = jnp.concatenate([w1, bias_cols], axis=1)
-    cols = lax.dynamic_slice_in_dim(theta_second, shell * outs, outs, 2)
-    w2 = jnp.einsum("kio,hg->khogi", cols, eye).reshape(degrees * 2 * outs, 2 * channels)
-
     ext = exchange(density, kernel_table, shell_row)
     half = rows // 2
     need = half + 2 * (degrees - 1)
     vmem = pl.BlockSpec(memory_space=pltpu.VMEM)
     return pl.pallas_call(
-        functools.partial(conv_kernel, degrees),
+        conv_kernel,
         out_shape=jax.ShapeDtypeStruct((outs, rows, width), jnp.bfloat16),
-        in_specs=[vmem, vmem, vmem, pl.BlockSpec(memory_space=pltpu.SMEM)],
+        in_specs=[pl.BlockSpec(memory_space=pl.ANY), vmem, vmem, vmem, pl.BlockSpec(memory_space=pltpu.SMEM)],
         out_specs=vmem,
         scratch_shapes=[
+            pltpu.VMEM(ext.shape, ext.dtype),
             pltpu.VMEM((degrees, half + 2 * EDGE, 2 * bins, width), jnp.float32),
             pltpu.VMEM((degrees, need, 2 * outs, width), jnp.float32),
             pltpu.VMEM((outs, rows, width), jnp.float32),
+            pltpu.VMEM((2 * bins * degrees + 16, 2 * channels), jnp.float32),
+            pltpu.VMEM((degrees, channels, 2 * channels), jnp.float32),
+            pltpu.SemaphoreType.DMA,
         ],
-        compiler_params=pltpu.CompilerParams(vmem_limit_bytes=40 * 2**20),
-    )(ext, w1, w2, bias_second)
+        compiler_params=pltpu.CompilerParams(vmem_limit_bytes=58 * 2**20),
+    )(ext, theta_first, bias_first.reshape(1, channels), theta_second, bias_second)
 
 
 def solution(mesh):

time: 30.5 us -> 27.4 us (0.90)
  local copies, waits for them, and re-layouts: 3.55 us -> 0 us
  Pallas kernels: 26.1 us -> 27.2 us
  other arithmetic: 0.44 us -> 0 us
    unnamed x12 -> x0, local copies, waits for them, and re-layouts: 2.12 us -> none
    pallas_call x1, Pallas kernels: 7.57 us -> 8.92 us  [per_device(): pl.pallas_call(conv_kernel, out_shape=jax.ShapeDtypeStruct((outs, rows, w...]
    reduce_precision x1 -> x0, local copies, waits for them, and re-layouts: 0.68 us -> none  [exchange(): lax.reduce_precision(kernel_table, 8, 7)]
    reshape x3 -> x0, local copies, waits for them, and re-layouts: 0.31 us -> none  [the longest x2 0.21 us: per_device(): jnp.einsum('kbo,hg->hokgb', theta_first, eye)]
where the time goes in v3:
time: 27.4 us; the launch traced here: 27.2 us
  Pallas kernels  27.2 us (99%)
    pallas_call x1, Pallas kernels, exchange(): pl.pallas_call(functools.partial(exchange_kernel, groups, tiles), out_sha...  18.3 us
    pallas_call x1, Pallas kernels, per_device(): pl.pallas_call(conv_kernel, out_shape=jax.ShapeDtypeStruct((outs, rows, w...  8.92 us

profile of v3, /device:TPU:0, one launch (start us, length us, event | category | flops | bytes accessed | tf_op | source)
XLA Modules:
  0.0 27.2 jit_solution(14866815144172633318)
XLA Ops:
  0.0 18.3 %shard_map.73.ext_hbm = bf16[4,80,384]{2,1,0:T(8,128)(2,1)} custom-call(bf16[25,48,384]{2,1,0:T(8,128)(2,1)} %density_hbm.1, f32[4,16]{1,0:T(4,128)} %bitcast.2, s32[25]{0:T(128)} %row_ref.1), custom_call_target="tpu_custom_call" | custom-call | flops 3686400 | bytes 921600 | tf_op jit(solution)/shard_map/pallas_call | solution.py:126
  18.3 8.9 %shard_map.74 = bf16[16,48,384]{2,1,0:T(8,128)(2,1)} custom-call(bf16[4,80,384]{2,1,0:T(8,128)(2,1)} %shard_map.73.ext_hbm, bf16[6,4,64]{2,1,0:T(4,128)(2,1)} %first_ref.1, f32[1,64]{1,0:T(1,128)} %bitcast.3, bf16[6,64,64]{2,1,0:T(8,128)(2,1)} %second_ref.1, f32[64]{0:T(128)} %bias_ref.1), custom_call_target="tpu_custom_call" | custom-call | tf_op jit(solution)/shard_map/pallas_call | solution.py:279

commit v4 on v3

--- a/solution.py
+++ b/solution.py
@@ -9,8 +9,6 @@
 
 MESH = pl.DeviceIdType.MESH
 EDGE = 16
-CL = 1
-MIXU = True
 
 
 def exchange_kernel(
@@ -125,7 +123,7 @@
     chunks = rows // EDGE
     return pl.pallas_call(
         functools.partial(exchange_kernel, groups, tiles),
-        out_shape=jax.ShapeDtypeStruct((bins, rows + 2 * EDGE, width), jnp.bfloat16),
+        out_shape=pltpu.VMEM((bins, rows + 2 * EDGE, width), jnp.bfloat16),
         in_specs=[
             pl.BlockSpec(memory_space=pl.ANY),
             pl.BlockSpec(memory_space=pltpu.SMEM),
@@ -147,9 +145,7 @@
     )(density, kernel_table.T, shell_row)
 
 
-def conv_kernel(ext_hbm, first_ref, lift_ref, second_ref, bias_ref, out_ref, ext_ref, basis, mixed, result, flat_first, turned, sem):
-    load = pltpu.make_async_copy(ext_hbm, ext_ref, sem)
-    load.start()
+def conv_kernel(ext_ref, first_ref, lift_ref, second_ref, bias_ref, out_ref, basis, mixed, result, flat_first, turned):
     degrees, bins, channels = first_ref.shape
     width = ext_ref.shape[2]
     shell = lax.axis_index("shell")
@@ -182,7 +178,6 @@
         pieces.append(jnp.where(lanes < channels, mine, 0.0))
         pieces.append(jnp.where(lanes < channels, 0.0, mine))
     w2 = jnp.concatenate(pieces, axis=0).astype(jnp.bfloat16)
-    load.wait()
 
     def lateral(field):
         flat = field.reshape(-1, width)
@@ -216,7 +211,7 @@
     ones = jnp.ones((16, width), jnp.float32)
     deep = w2.shape[0] // degrees
 
-    def mix(pair, _):
+    def mix(pair):
         columns = []
         for q in range(2):
             row = base + 2 * pair + q
@@ -228,27 +223,15 @@
         for q in range(2):
             for k in range(degrees):
                 mixed[k, 2 * pair + q] = u[k * deep:(k + 1) * deep, q * width:(q + 1) * width]
-        return 0
-
-    lax.fori_loop(0, need // 2, mix, 0, unroll=MIXU)
-
-    for k in range(degrees - 2, 0, -1):
-        first = degrees - 1 - k
-
-        def clenshaw(r, n, k=k):
-            value = mixed[k, pl.ds(r, n)] - 0.5 * (
-                mixed[k + 1, pl.ds(r - 1, n)] + mixed[k + 1, pl.ds(r + 1, n)] + lateral(mixed[k + 1, pl.ds(r, n)]))
-            if k + 2 < degrees:
-                value = value - mixed[k + 2, pl.ds(r, n)]
-            mixed[k, pl.ds(r, n)] = value
-
-        count = need - 2 * first
-        for i in range(count // CL):
-            clenshaw(first + i * CL, CL)
-        if count % CL:
-            clenshaw(first + count // CL * CL, count % CL)
-
-    def finish(block, _):
+
+    def clenshaw(k, r):
+        total = mixed[k + 1, r - 1] + mixed[k + 1, r + 1] + lateral(mixed[k + 1, r])
+        value = mixed[k, r] - 0.5 * total
+        if k + 2 < degrees:
+            value = value - mixed[k + 2, r]
+        mixed[k, r] = value
+
+    def finish(block):
         values = []
         for i in range(8):
             r = reach + block * 8 + i
@@ -256,11 +239,22 @@
             values.append(mixed[0, r] - 0.25 * total - mixed[2, r])
         stacked = jnp.stack(values)
         for h in range(2):
-            start = pl.multiple_of(h * half + block * 8, 8)
-            result[:, pl.ds(start, 8), :] = jnp.swapaxes(stacked[:, h * outs:(h + 1) * outs], 0, 1)
-        return 0
-
-    lax.fori_loop(0, half // 8, finish, 0)
+            start = h * half + block * 8
+            result[:, start:start + 8, :] = jnp.swapaxes(stacked[:, h * outs:(h + 1) * outs], 0, 1)
+
+    ready = {k: reach - k for k in range(degrees)}
+    finished = 0
+    for pair in range(need // 2):
+        mix(pair)
+        ready[reach] = 2 * pair + 2
+        for k in range(reach - 1, 0, -1):
+            while ready[k] + 1 < ready[k + 1]:
+                clenshaw(k, ready[k])
+                ready[k] += 1
+        while finished < half // 8 and reach + finished * 8 + 8 < ready[1]:
+            finish(finished)
+            finished += 1
+
     for o in range(outs):
         out_ref[o] = (result[o] + bias_ref[shell * outs + o]).astype(jnp.bfloat16)
 
@@ -279,18 +273,16 @@
     return pl.pallas_call(
         conv_kernel,
         out_shape=jax.ShapeDtypeStruct((outs, rows, width), jnp.bfloat16),
-        in_specs=[pl.BlockSpec(memory_space=pl.ANY), vmem, vmem, vmem, pl.BlockSpec(memory_space=pltpu.SMEM)],
+        in_specs=[vmem, vmem, vmem, vmem, pl.BlockSpec(memory_space=pltpu.SMEM)],
         out_specs=vmem,
         scratch_shapes=[
-            pltpu.VMEM(ext.shape, ext.dtype),
             pltpu.VMEM((degrees, half + 2 * EDGE, 2 * bins, width), jnp.float32),
             pltpu.VMEM((degrees, need, 2 * outs, width), jnp.float32),
             pltpu.VMEM((outs, rows, width), jnp.float32),
             pltpu.VMEM((2 * bins * degrees + 16, 2 * channels), jnp.float32),
             pltpu.VMEM((degrees, channels, 2 * channels), jnp.float32),
-            pltpu.SemaphoreType.DMA,
         ],
-        compiler_params=pltpu.CompilerParams(vmem_limit_bytes=58 * 2**20),
+        compiler_params=pltpu.CompilerParams(vmem_limit_bytes=28 * 2**20),
     )(ext, theta_first, bias_first.reshape(1, channels), theta_second, bias_second)
 
 

time: 27.4 us -> 26 us (0.949)
  Pallas kernels: 27.2 us -> 25.8 us
    pallas_call x1, Pallas kernels: 8.92 us -> 8.03 us  [per_device(): pl.pallas_call(conv_kernel, out_shape=jax.ShapeDtypeStruct((outs, rows, w...]
    pallas_call x1, Pallas kernels: 18.3 us -> 17.7 us  [exchange(): pl.pallas_call(functools.partial(exchange_kernel, groups, tiles), out_sha...]
where the time goes in v4:
time: 26 us; the launch traced here: 25.8 us
  Pallas kernels  25.8 us (99%)
    pallas_call x1, Pallas kernels, exchange(): pl.pallas_call(functools.partial(exchange_kernel, groups, tiles), out_sha...  17.7 us
    pallas_call x1, Pallas kernels, per_device(): pl.pallas_call(conv_kernel, out_shape=jax.ShapeDtypeStruct((outs, rows, w...  8.03 us

profile of v4, /device:TPU:0, one launch (start us, length us, event | category | flops | bytes accessed | tf_op | source)
XLA Modules:
  0.0 25.8 jit_solution(1790019458544062063)
XLA Ops:
  0.0 0.0 copy-start
  0.0 0.0 copy-start.1
  0.0 0.0 copy-start.2
  0.0 0.0 copy-start.3
  0.0 17.7 %shard_map.73.ext_ref = bf16[4,80,384]{2,1,0:T(8,128)(2,1)S(1)} custom-call(bf16[25,48,384]{2,1,0:T(8,128)(2,1)} %density_hbm.1, f32[4,16]{1,0:T(4,128)} %bitcast.3, s32[25]{0:T(128)} %row_ref.1), custom_call_target="tpu_custom_call" | custom-call | flops 3686400 | bytes 921600 | tf_op jit(solution)/shard_map/pallas_call | solution.py:124
  17.7 0.0 copy-done
  17.7 0.0 copy-done.1
  17.8 0.0 copy-done.2
  17.8 0.0 copy-done.3
  17.8 8.0 %shard_map.74 = bf16[16,48,384]{2,1,0:T(8,128)(2,1)} custom-call(bf16[4,80,384]{2,1,0:T(8,128)(2,1)S(1)} %shard_map.73.ext_ref, bf16[6,4,64]{2,1,0:T(4,128)(2,1)S(1)} %copy-done.1, f32[1,64]{1,0:T(1,128)S(1)} %bitcast.2, bf16[6,64,64]{2,1,0:T(8,128)(2,1)S(1)} %copy-done, f32[64]{0:T(128)S(1)} %copy-done.3), custom_call_target="tpu_custom_call" | custom-call | tf_op jit(solution)/shard_map/pallas_call | solution.py:273
Async XLA Ops:
  0.0 17.7 %copy-start = (bf16[6,64,64]{2,1,0:T(8,128)(2,1)S(1)}, bf16[6,64,64]{2,1,0:T(8,128)(2,1)}, u32[]{:S(2)}) copy-start(bf16[6,64,64]{2,1,0:T(8,128)(2,1)} %second_ref.1) | copy-start | bytes 147460
  0.0 17.7 %copy-start.1 = (bf16[6,4,64]{2,1,0:T(4,128)(2,1)S(1)}, bf16[6,4,64]{2,1,0:T(4,128)(2,1)}, u32[]{:S(2)}) copy-start(bf16[6,4,64]{2,1,0:T(4,128)(2,1)} %first_ref.1) | copy-start | bytes 9220
  0.0 17.8 %copy-start.2 = (f32[64]{0:T(128)S(1)}, f32[64]{0:T(128)}, u32[]{:S(2)}) copy-start(f32[64]{0:T(128)} %param.11) | copy-start | bytes 772
  0.0 17.8 %copy-start.3 = (f32[64]{0:T(128)S(1)}, f32[64]{0:T(128)}, u32[]{:S(2)}) copy-start(f32[64]{0:T(128)} %bias_ref.1) | copy-start | bytes 772
